TPU v7x, 32 devices: a whole 2x2x4 slice. The times are simulated.
32 devices in a mesh: groups: 2 (over y), dp: 4 (over z), tensor: 4 (over x, core).
Axes of the slice: x: 2, y: 2, z: 4, core: 2. Of those that a mesh axis runs over, the one named last changes fastest.
Arguments:
- residual: bfloat16 [8192, 8192], P(('groups', 'dp'), 'tensor'), parts along dimension 0, may hold values from -128 to 128, as said below
- norm_gain: float32 [8192], P('tensor'), may hold values from 0.5 to 1.5
- key_weight: bfloat16 [8192, 512], P('tensor'), may hold values from -0.0625 to 0.0625
- value_weight: bfloat16 [8192, 512], P('tensor'), may hold values from -0.0625 to 0.0625
- key_grad: bfloat16 [8192, 512], P(('groups', 'dp', 'tensor')), parts along dimension 0, may hold values from -6 to 6
- value_grad: bfloat16 [8192, 512], P(('groups', 'dp', 'tensor')), parts along dimension 0, may hold values from -6 to 6
- key_left: bfloat16 [8192, 64], P('tensor'), may hold values from -0.0625 to 0.0625
- value_left: bfloat16 [8192, 64], P('tensor'), may hold values from -0.0625 to 0.0625
- key_right: bfloat16 [512, 64], replicated, may hold values from -0.25 to 0.25
- value_right: bfloat16 [512, 64], replicated, may hold values from -0.25 to 0.25
- queries: bfloat16 [64, 8192], P(('dp', 'tensor')), may hold values from -1.5 to 1.5
- doc_lengths: int32 [8], P(('groups', 'dp')), parts along dimension 0, may hold values from 128 to 1024
Outputs:
- key_out: bfloat16 [8192, 512], P(('groups', 'dp', 'tensor')), parts along dimension 0
- value_out: bfloat16 [8192, 512], P(('groups', 'dp', 'tensor')), parts along dimension 0
- hidden_grad: bfloat16 [8192, 8192], P(('groups', 'dp'), 'tensor'), parts along dimension 0
- scores: float32 [8, 64], P('groups', ('dp', 'tensor')), parts along dimension 0
There are 2 independent parts, one for each index of `groups`. A program takes and returns all parts, laid end to end along the dimension named above; an argument that names none is the same for every part. Nothing has to cross between parts.
Inputs may be any that keep to these rules, and one draw needn't show every extreme that they name: `residual`: each entry is a token's feature; padding slots hold numbers too. `doc_lengths`: the number of leading slots of each document that hold tokens; the rest are padding.
All inputs are finite; a program needn't handle non-finite values.
Results may differ from a plain program's by a relative error of at most 0.019.
Values may be sent and summed in bfloat16 or wider, within the bound.
A program may use at most 64 MiB of HBM per device.

v0:
```python
import jax
import jax.numpy as jnp
from jax import lax
from jax.sharding import PartitionSpec as P

TOK_DEV = 1024


def gram_part(left_rows, right_rows):
    return lax.dot_general(
        left_rows,
        right_rows,
        (((0,), (0,)), ((), ())),
        precision=lax.Precision.HIGHEST,
        preferred_element_type=jnp.float32,
    )


def body(
    residual,
    norm_gain,
    key_weight,
    value_weight,
    key_grad,
    value_grad,
    key_left,
    value_left,
    key_right,
    value_right,
    queries,
    doc_lengths,
):
    parts = lax.axis_size("tensor")
    own_index = lax.axis_index("tensor")
    widened = residual.astype(jnp.float32)
    width = widened.shape[1] * parts
    square_sum = lax.psum(jnp.sum(widened * widened, axis=1), "tensor")
    inverse = lax.rsqrt(square_sum / width + 1e-05)[:, None]
    normed = (widened * inverse * norm_gain).astype(jnp.bfloat16)
    columns = key_weight.shape[1]
    own_rows = key_grad.shape[0]
    pieces = [
        jnp.dot(normed, key_weight, preferred_element_type=jnp.float32),
        jnp.dot(normed, value_weight, preferred_element_type=jnp.float32),
    ]
    summed = lax.psum_scatter(
        jnp.concatenate(pieces, axis=1).astype(jnp.bfloat16),
        "tensor",
        scatter_dimension=0,
        tiled=True,
    ).astype(jnp.float32)
    key_out = summed[:, :columns].astype(jnp.bfloat16)
    value_out = summed[:, columns : 2 * columns].astype(jnp.bfloat16)
    slots = own_index * own_rows + jnp.arange(own_rows, dtype=jnp.int32)
    live = (slots < doc_lengths[0]).astype(jnp.bfloat16)[:, None]
    key_own = key_grad * live
    value_own = value_grad * live
    key_masked, value_masked = (
        lax.all_gather(key_own, "tensor", axis=0, tiled=True),
        lax.all_gather(value_own, "tensor", axis=0, tiled=True),
    )
    contract = (((1,), (1,)), ((), ()))
    back = lax.dot_general(key_masked, key_weight, contract, preferred_element_type=jnp.float32)
    back = back + lax.dot_general(
        value_masked, value_weight, contract, preferred_element_type=jnp.float32
    )
    hidden_grad = back.astype(jnp.bfloat16)
    key_first = jnp.dot(normed, key_left, preferred_element_type=jnp.float32)
    value_first = jnp.dot(normed, value_left, preferred_element_type=jnp.float32)
    key_first, value_first = (
        lax.psum(key_first.astype(jnp.bfloat16), "tensor").astype(jnp.float32),
        lax.psum(value_first.astype(jnp.bfloat16), "tensor").astype(jnp.float32),
    )
    key_second = jnp.dot(key_masked, key_right, preferred_element_type=jnp.float32)
    value_second = jnp.dot(value_masked, value_right, preferred_element_type=jnp.float32)
    key_gram = gram_part(key_first, key_second)
    value_gram = gram_part(value_first, value_second)
    flat = jnp.concatenate(
        [(key_gram / TOK_DEV).reshape(-1), (value_gram / TOK_DEV).reshape(-1)]
    ).astype(jnp.bfloat16)
    every_doc = lax.all_gather(flat[None, :], "dp", axis=0, tiled=True)
    scores = lax.dot_general(
        every_doc, queries, (((1,), (1,)), ((), ())), preferred_element_type=jnp.float32
    )
    return (key_out, value_out, hidden_grad, scores)


def solution(mesh):
    in_specs = (
        P(("groups", "dp"), "tensor"),
        P("tensor"),
        P("tensor", None),
        P("tensor", None),
        P(("groups", "dp", "tensor"), None),
        P(("groups", "dp", "tensor"), None),
        P("tensor", None),
        P("tensor", None),
        P(),
        P(),
        P(("dp", "tensor"), None),
        P(("groups", "dp")),
    )
    out_specs = (
        P(("groups", "dp", "tensor"), None),
        P(("groups", "dp", "tensor"), None),
        P(("groups", "dp"), "tensor"),
        P("groups", ("dp", "tensor")),
    )
    return jax.shard_map(body, mesh=mesh, in_specs=in_specs, out_specs=out_specs, check_vma=False)
```

profile of v0, /device:TPU:0, one launch (start us, length us, event | category | flops | bytes accessed | tf_op | source)
XLA Modules:
  0.0 126.5 jit_solution(11898693926931286711)
XLA Ops:
  7.2 0.0 copy-start
  7.2 0.0 copy-start.8
  7.2 0.0 all-gather.6.cloned.1.call-start
  8.0 1.9 %broadcast_multiply_fusion = (bf16[256,512]{1,0:T(8,128)(2,1)}, bf16[256,512]{1,0:T(8,128)(2,1)}) fusion(bf16[256,512]{1,0:T(8,128)(2,1)} %param.17, bf16[256]{0:T(256)(128)(2,1)S(1)} %compare_convert_fusion, bf16[256,512]{1,0:T(8,128)(2,1)} %param.16), kind=kLoop, calls=%fused_computation.15 | loop fusion | flops 262144 | bytes 1049088 | tf_op jit(solution)/shard_map/mul | solution.py:57
  10.0 0.0 all-gather.6.cloned.1.call-update
  10.0 0.0 all-reduce.3.cloned.1.call-start
  10.0 3.1 %fusion = f32[1024]{0:T(1024)S(1)} fusion(bf16[1024,2048]{1,0:T(8,128)(2,1)} %param.12), kind=kLoop, calls=%fused_computation.2 | loop fusion | flops 6290432 | bytes 4198400 | tf_op jit(solution)/shard_map/reduce_sum | solution.py:37
  13.1 8.3 %psum.21 = f32[1024]{0:T(1024)S(1)} all-reduce(f32[1024]{0:T(1024)S(1)} %fusion), channel_id=1, replica_groups=mesh['groups'=2,'dp'=4,'tensor'=4] {'tensor'}, use_global_device_ids=true, to_apply=%region_1.0 | all-reduce | flops 1024 | bytes 8192 | tf_op jit(solution)/shard_map/psum | solution.py:37
  21.5 0.0 copy-done.8
  21.5 0.0 copy-start.4
  21.5 3.3 %fusion.2 = bf16[1024,2048]{1,0:T(8,128)(2,1)S(1)} fusion(bf16[1024,2048]{1,0:T(8,128)(2,1)} %param.12, f32[2048]{0:T(1024)S(1)} %copy-done.8, f32[1024]{0:T(1024)S(1)} %add_rsqrt_fusion), kind=kLoop, calls=%fused_computation.4 | loop fusion | flops 8388608 | bytes 8400896 | tf_op jit(solution)/shard_map/convert_element_type | solution.py:39
  24.7 0.0 copy-done.4
  24.7 0.0 copy-start.1
  24.8 0.0 copy-start.5
  24.8 2.1 %convolution_convert_fusion.2 = bf16[1024,64]{0,1:T(8,128)(2,1)} fusion(bf16[1024,2048]{1,0:T(8,128)(2,1)S(1)} %fusion.2, bf16[2048,64]{0,1:T(8,128)(2,1)S(1)} %copy-done.4), kind=kOutput, calls=%fused_computation.9 | convolution fusion | flops 268500992 | bytes 4587520 | tf_op jit(solution)/shard_map/dot_general | solution.py:69
  26.9 0.0 copy-done.1
  26.9 0.0 copy-done.5
  26.9 2.0 %convolution_convert_fusion.3 = bf16[1024,64]{0,1:T(8,128)(2,1)} fusion(bf16[1024,2048]{1,0:T(8,128)(2,1)S(1)} %fusion.2, bf16[2048,64]{0,1:T(8,128)(2,1)S(1)} %copy-done.5), kind=kOutput, calls=%fused_computation.10 | convolution fusion | flops 268500992 | bytes 4587520 | tf_op jit(solution)/shard_map/dot_general | solution.py:68
  28.9 0.0 all-reduce.3.cloned.1.call-update
  29.0 0.0 all-gather.4.cloned.1.call-start
  29.0 0.7 all-gather.4.cloned.1.call-update
  29.7 0.0 reduce-scatter.2.cloned.1.call-start
  29.7 0.0 copy-start.2
  29.8 5.4 %convolution_convert_fusion = bf16[1024,512]{0,1:T(8,128)(2,1)S(1)} fusion(bf16[1024,2048]{1,0:T(8,128)(2,1)} %copy-done.1, bf16[2048,512]{1,0:T(8,128)(2,1)} %param.15), kind=kOutput, calls=%fused_computation.7 | convolution fusion | flops 2148007936 | bytes 7340032 | tf_op jit(solution)/shard_map/dot_general | solution.py:44
  35.1 0.0 copy-done
  35.1 2.4 %convolution_convert_fusion.1 = bf16[1024,512]{0,1:T(8,128)(2,1)S(1)} fusion(bf16[1024,2048]{1,0:T(8,128)(2,1)S(1)} %copy-done.2, bf16[2048,512]{1,0:T(8,128)(2,1)S(1)} %copy-done), kind=kOutput, calls=%fused_computation.8 | convolution fusion | flops 2148007936 | bytes 7340032 | tf_op jit(solution)/shard_map/dot_general | solution.py:43
  37.6 0.0 copy-start.6
  37.6 0.0 copy-start.7
  37.6 0.0 copy-start.10
  37.6 1.5 %pad_maximum_fusion = bf16[1024,1024]{0,1:T(8,128)(2,1)} fusion(bf16[1024,512]{0,1:T(8,128)(2,1)S(1)} %convolution_convert_fusion, bf16[1024,512]{0,1:T(8,128)(2,1)S(1)} %convolution_convert_fusion.1), kind=kLoop, calls=%fused_computation.6 | loop fusion | flops 4194304 | bytes 4194304 | tf_op jit(solution)/shard_map/concatenate | solution.py:47
  39.1 0.0 reduce-scatter.2.cloned.1.call-update
  39.1 0.0 all-gather.6.cloned.1.call-done
  39.2 1.7 %fusion.11 = f32[1024,64]{0,1:T(8,128)S(1)} fusion(bf16[1024,512]{1,0:T(8,128)(2,1)} %all-gather.6.cloned.1.call-done, bf16[512,64]{0,1:T(8,128)(2,1)S(1)} %copy-done.6), kind=kOutput, calls=%fused_computation.26 | convolution fusion | flops 67108864 | bytes 1376256 | tf_op jit(solution)/shard_map/dot_general | solution.py:75
  40.8 23.4 %all-reduce.3.cloned.1.call-done = (bf16[1024,64]{0,1:T(8,128)(2,1)}, bf16[1024,64]{0,1:T(8,128)(2,1)}) async-done(((bf16[1024,64]{0,1:T(8,128)(2,1)}, bf16[1024,64]{0,1:T(8,128)(2,1)}), (bf16[1024,64]{0,1:T(8,128)(2,1)}, bf16[1024,64]{0,1:T(8,128)(2,1)})) %all-reduce.3.cloned.1.call-update) | async-done | bytes 262160 | tf_op jit(solution)/shard_map/psum | solution.py:72
  64.2 1.2 fusion.4
  65.4 0.1 concatenate.21
  65.5 17.7 %all-gather.4.cloned.1.call-done = bf16[1024,512]{1,0:T(8,128)(2,1)} async-done(((bf16[256,512]{1,0:T(8,128)(2,1)}), bf16[1024,512]{1,0:T(8,128)(2,1)}) %all-gather.4.cloned.1.call-update) | async-done | bytes 1048592 | tf_op jit(solution)/shard_map/all_gather | solution.py:59
  83.2 1.7 %fusion.10 = f32[1024,64]{0,1:T(8,128)S(1)} fusion(bf16[1024,512]{1,0:T(8,128)(2,1)} %all-gather.4.cloned.1.call-done, bf16[512,64]{0,1:T(8,128)(2,1)S(1)} %copy-done.7), kind=kOutput, calls=%fused_computation.25 | convolution fusion | flops 67108864 | bytes 1376256 | tf_op jit(solution)/shard_map/dot_general | solution.py:74
  84.9 1.2 fusion.3
  86.1 0.1 concatenate.20
  86.2 13.6 %all-gather = bf16[4,1,8192]{2,1,0:T(2,128)(2,1)S(1)} all-gather(bf16[1,1,8192]{2,1,0:T(2,128)(2,1)S(1)} %maximum_bitcast_fusion), channel_id=1, replica_groups=mesh['groups'=2,'dp'=4,'tensor'=4] {'dp'}, dimensions={0}, use_global_device_ids=true | all-gather | bytes 81920 | tf_op jit(solution)/shard_map/all_gather | solution.py:81
  99.8 0.8 fusion.5
  100.6 3.7 %fusion.9 = f32[1024,2048]{1,0:T(8,128)S(1)} fusion(bf16[1024,512]{1,0:T(8,128)(2,1)} %all-gather.4.cloned.1.call-done, bf16[2048,512]{1,0:T(8,128)(2,1)S(1)} %copy-done), kind=kOutput, calls=%fused_computation.24 | convolution fusion | flops 2147483648 | bytes 11534336 | tf_op jit(solution)/shard_map/dot_general | solution.py:63
  104.4 4.4 %add_convert_fusion = bf16[1024,2048]{1,0:T(8,128)(2,1)} fusion(f32[1024,2048]{1,0:T(8,128)S(1)} %fusion.9, bf16[1024,512]{1,0:T(8,128)(2,1)S(1)} %copy-done.3, bf16[2048,512]{1,0:T(8,128)(2,1)S(1)} %copy-done.9), kind=kOutput, calls=%fused_computation.5 | convolution fusion | flops 2151677952 | bytes 15728640 | tf_op jit(solution)/shard_map/dot_general | solution.py:64
  108.7 8.5 %reduce-scatter.2.cloned.1.call-done = bf16[256,1024]{0,1:T(8,128)(2,1)} async-done(((bf16[1024,1024]{0,1:T(8,128)(2,1)}), bf16[256,1024]{0,1:T(8,128)(2,1)}) %reduce-scatter.2.cloned.1.call-update) | async-done | bytes 524304 | tf_op jit(solution)/shard_map/reduce_scatter | solution.py:46
  117.2 1.1 fusion.8
  118.3 0.8 copy.21
  119.1 0.8 copy.20
  (11 shorter events, 0.1 us)
Async XLA Ops:
  7.2 28.0 %copy-start = (bf16[2048,512]{1,0:T(8,128)(2,1)S(1)}, bf16[2048,512]{1,0:T(8,128)(2,1)}, u32[]{:S(2)}) copy-start(bf16[2048,512]{1,0:T(8,128)(2,1)} %param.14) | copy-start | bytes 6291460
  7.2 14.3 %copy-start.8 = (f32[2048]{0:T(1024)S(1)}, f32[2048]{0:T(1024)}, u32[]{:S(2)}) copy-start(f32[2048]{0:T(1024)} %param.13) | copy-start | bytes 24580
  7.2 32.0 %all-gather.6.cloned.1.call-start = ((), (), s32[]{:S(2)}) async-start(), calls=%async_computation.3 | async-start | bytes 1310720 | tf_op jit(solution)/shard_map/all_gather | solution.py:60
  10.0 54.2 %all-reduce.3.cloned.1.call-start = ((), (), s32[]{:S(2)}) async-start(), calls=%async_computation.4 | async-start | bytes 524288 | tf_op jit(solution)/shard_map/psum | solution.py:72
  21.5 3.3 %copy-start.4 = (bf16[2048,64]{0,1:T(8,128)(2,1)S(1)}, bf16[2048,64]{0,1:T(8,128)(2,1)}, u32[]{:S(2)}) copy-start(bf16[2048,64]{0,1:T(8,128)(2,1)} %param.19) | copy-start | bytes 786436
  24.7 2.1 %copy-start.1 = (bf16[1024,2048]{1,0:T(8,128)(2,1)}, bf16[1024,2048]{1,0:T(8,128)(2,1)S(1)}, u32[]{:S(2)}) copy-start(bf16[1024,2048]{1,0:T(8,128)(2,1)S(1)} %fusion.2) | copy-start | bytes 12582916
  24.8 2.1 %copy-start.5 = (bf16[2048,64]{0,1:T(8,128)(2,1)S(1)}, bf16[2048,64]{0,1:T(8,128)(2,1)}, u32[]{:S(2)}) copy-start(bf16[2048,64]{0,1:T(8,128)(2,1)} %param.18) | copy-start | bytes 786436
  29.0 54.2 %all-gather.4.cloned.1.call-start = ((), (), s32[]{:S(2)}) async-start(), calls=%async_computation.2 | async-start | bytes 1310720 | tf_op jit(solution)/shard_map/all_gather | solution.py:59
  29.7 87.5 %reduce-scatter.2.cloned.1.call-start = ((), (), s32[]{:S(2)}) async-start(), calls=%async_computation.1 | async-start | bytes 2621440 | tf_op jit(solution)/shard_map/reduce_scatter | solution.py:46
  29.7 5.4 %copy-start.2 = (bf16[1024,2048]{1,0:T(8,128)(2,1)S(1)}, bf16[1024,2048]{1,0:T(8,128)(2,1)}, u32[]{:S(2)}) copy-start(bf16[1024,2048]{1,0:T(8,128)(2,1)} %copy-done.1) | copy-start | bytes 12582916
  37.6 1.6 %copy-start.6 = (bf16[512,64]{0,1:T(8,128)(2,1)S(1)}, bf16[512,64]{0,1:T(8,128)(2,1)}, u32[]{:S(2)}) copy-start(bf16[512,64]{0,1:T(8,128)(2,1)} %param.21) | copy-start | bytes 196612
  37.6 45.6 %copy-start.7 = (bf16[512,64]{0,1:T(8,128)(2,1)S(1)}, bf16[512,64]{0,1:T(8,128)(2,1)}, u32[]{:S(2)}) copy-start(bf16[512,64]{0,1:T(8,128)(2,1)} %param.20) | copy-start | bytes 196612
  37.6 62.2 %copy-start.10 = (bf16[4,8192]{1,0:T(4,128)(2,1)S(1)}, bf16[4,8192]{1,0:T(4,128)(2,1)}, u32[]{:S(2)}) copy-start(bf16[4,8192]{1,0:T(4,128)(2,1)} %param.22) | copy-start | bytes 196612
  100.6 3.8 %copy-start.3 = (bf16[1024,512]{1,0:T(8,128)(2,1)S(1)}, bf16[1024,512]{1,0:T(8,128)(2,1)}, u32[]{:S(2)}) copy-start(bf16[1024,512]{1,0:T(8,128)(2,1)} %all-gather.6.cloned.1.call-done) | copy-start | bytes 3145732
  100.6 3.8 %copy-start.9 = (bf16[2048,512]{1,0:T(8,128)(2,1)S(1)}, bf16[2048,512]{1,0:T(8,128)(2,1)}, u32[]{:S(2)}) copy-start(bf16[2048,512]{1,0:T(8,128)(2,1)} %param.15) | copy-start | bytes 6291460
Sparse Core Ops, SparseCore 0:
  10.2 19.4 all-gather.5
  32.0 32.1 all-reduce.2
  66.4 16.7 all-gather.3
  85.7 31.4 reduce-scatter.1
where the time goes:
time: 127 us
  waiting for transfers between devices  50.3 us (40%)
  matrix products  26.5 us (21%)
  blocking collectives  21.9 us (17%)
  between operations  14.7 us (12%)
  other arithmetic  9.81 us (8%)
  local copies, waits for them, and re-layouts  2.99 us (2%)
    psum x1, waiting for transfers between devices, body(): lax.psum(value_first.astype(jnp.bfloat16), 'tensor').astype(jnp.float32)  23.4 us
    all_gather x1, waiting for transfers between devices, body(): lax.all_gather(key_own, 'tensor', axis=0, tiled=True)  17.7 us
    all_gather x1, blocking collectives, body(): every_doc = lax.all_gather(flat[None, :], 'dp', axis=0, tiled=True)  13.6 us
    reduce_scatter x1, waiting for transfers between devices, body(): lax.psum_scatter(jnp.concatenate(pieces, axis=1).astype(jnp.bfloat16), 't...  8.47 us
    psum x1, blocking collectives, body(): square_sum = lax.psum(jnp.sum(widened * widened, axis=1), 'tensor')  8.35 us
    dot_general x1, matrix products, body(): jnp.dot(normed, value_weight, preferred_element_type=jnp.float32)  5.37 us
    dot_general x1, matrix products, body(): lax.dot_general(value_masked, value_weight, contract, preferred_element_t...  4.38 us
    dot_general x1, matrix products, body(): lax.dot_general(key_masked, key_weight, contract, preferred_element_type=...  3.74 us
  transfers between devices with their start and end apart: 4, of which 3 were waited for; matrix products, arithmetic and copies ran while one was open for 27% of the time, Pallas kernels for 0%

commit v1 on v0

v1 whole, which is shorter than its diff:
```python
import functools

import jax
import jax.numpy as jnp
from jax import lax
from jax.experimental import pallas as pl
from jax.experimental.pallas import tpu as pltpu
from jax.sharding import PartitionSpec as P

F32, BF16 = jnp.float32, jnp.bfloat16
LANES = 128


def kernel(
    parts,
    docs,
    residual,
    gain,
    key_weight,
    value_weight,
    key_grad,
    value_grad,
    key_left,
    value_left,
    key_right,
    value_right,
    queries,
    length,
    key_out,
    value_out,
    hidden_out,
    score_out,
    res_v,
    gain_v,
    kw_v,
    vw_v,
    kl_v,
    vl_v,
    left_w,
    kr_v,
    vr_v,
    got_k,
    got_v,
    mask_k,
    mask_v,
    partial,
    sib_in,
    x_out,
    x_in,
    left_t,
    squares,
    gram_rows,
    gram_in,
    flat_in,
    hid_v,
    load_sem,
    res_sem,
    own_sem,
    hid_sem,
    ag_sib_s,
    ag_sib_r,
    ag_x_s,
    ag_x_r,
    ag_f_s,
    ag_f_r,
    rs_sib_s,
    rs_sib_r,
    rs_x_s,
    rs_x_r,
    sq_s,
    sq_r,
    gr_s,
    gr_r,
    fl_s,
    fl_r,
):
    chips = parts // 2
    slots, features = res_v.shape
    rows = slots // parts
    columns = kw_v.shape[1]
    rank = kl_v.shape[1]
    me = lax.axis_index("tensor")
    doc = lax.axis_index("dp")
    chip, core = me // 2, lax.rem(me, 2)
    sibling = chip * 2 + 1 - core

    def send(src, dst, s_sem, r_sem, target):
        return pltpu.make_async_remote_copy(
            src_ref=src,
            dst_ref=dst,
            send_sem=s_sem,
            recv_sem=r_sem,
            device_id=target,
            device_id_type=pl.DeviceIdType.MESH,
        )

    def chip_at(step):
        return lax.rem(chip + step + chips, chips)

    def block_of(order):
        step = lax.rem(order // 2 + 1, chips)
        other = lax.rem(order, 2)
        return chip_at(step) * 2 + jnp.where(other == 0, 1 - core, core)

    loads = [
        pltpu.make_async_copy(src, dst, load_sem.at[i])
        for i, (src, dst) in enumerate(
            (
                (gain, gain_v),
                (key_weight, kw_v),
                (value_weight, vw_v),
                (key_left, kl_v),
                (value_left, vl_v),
                (key_right, kr_v),
                (value_right, vr_v),
            )
        )
    ]

    def res_copy(order):
        at = pl.ds(pl.multiple_of(block_of(order) * rows, rows), rows)
        return pltpu.make_async_copy(residual.at[at], res_v.at[at], res_sem.at[order])

    own_copies = [
        pltpu.make_async_copy(key_grad, got_k.at[me], own_sem.at[0]),
        pltpu.make_async_copy(value_grad, got_v.at[me], own_sem.at[1]),
    ]

    barrier = pltpu.get_barrier_semaphore()
    for step in range(1, parts):
        pl.semaphore_signal(
            barrier, inc=1, device_id={"tensor": lax.rem(me + step, parts)},
            device_id_type=pl.DeviceIdType.MESH,
        )

    def greet(step, carry):
        pl.semaphore_signal(
            barrier, inc=1, device_id={"dp": lax.rem(doc + step, docs)},
            device_id_type=pl.DeviceIdType.MESH,
        )
        return carry

    lax.fori_loop(1, docs, greet, 0)
    for copy in loads[:5]:
        copy.start()
    for order in range(parts):
        res_copy(order).start()
    for copy in loads[5:]:
        copy.start()
    for copy in own_copies:
        copy.start()
    pl.semaphore_wait(barrier, parts - 1 + docs - 1)

    grads = ((key_grad, got_k), (value_grad, got_v))
    ag_x = [
        [
            send(src, got.at[me], ag_x_s.at[step - 1, i], ag_x_r.at[step - 1, i],
                 {"tensor": chip_at(step) * 2 + core})
            for i, (src, got) in enumerate(grads)
        ]
        for step in range(1, chips)
    ]
    ag_sib = [
        send(src, got.at[me], ag_sib_s.at[i], ag_sib_r.at[i], {"tensor": sibling})
        for i, (src, got) in enumerate(grads)
    ]
    for pair in ag_x:
        for copy in pair:
            copy.start()
    for copy in ag_sib:
        copy.start()

    for copy in loads:
        copy.wait()
    left_w[:, :rank] = kl_v[...]
    left_w[:, rank:] = vl_v[...]

    def rs_sib(at):
        return send(partial.at[2 * at], sib_in.at[at], rs_sib_s.at[at], rs_sib_r.at[at],
                    {"tensor": sibling})

    def forward(order, carry):
        res_copy(order).wait()
        block = block_of(order)
        wide = res_v[pl.ds(pl.multiple_of(block * rows, rows), rows), :].astype(F32)
        scaled = (wide * gain_v[...]).astype(BF16)
        squared = wide * wide
        lane_sum = squared[:, :LANES]
        for i in range(1, features // LANES):
            lane_sum = lane_sum + squared[:, i * LANES : (i + 1) * LANES]
        squares[me, pl.ds(block, 1), :] = jnp.sum(lane_sum.T, axis=0, keepdims=True)
        partial[order, :, :columns] = jnp.dot(
            scaled, kw_v[...], preferred_element_type=F32
        ).astype(BF16)
        partial[order, :, columns:] = jnp.dot(
            scaled, vw_v[...], preferred_element_type=F32
        ).astype(BF16)
        left_t[block] = jnp.dot(scaled, left_w[...], preferred_element_type=F32).T

        @pl.when(lax.rem(order, 2) == 0)
        def _():
            rs_sib(order // 2).start()

        return carry

    lax.fori_loop(0, parts, forward, 0)

    sq = [
        send(squares.at[me], squares.at[me], sq_s.at[step - 1], sq_r.at[step - 1],
             {"tensor": lax.rem(me + step, parts)})
        for step in range(1, parts)
    ]
    for copy in sq:
        copy.start()

    rs_x = []
    for step in range(1, chips):
        at = step - 1
        rs_sib(at).wait_recv()
        x_out[at] = (
            partial[2 * at + 1].astype(F32) + sib_in[at].astype(F32)
        ).astype(BF16)
        rs_x.append(
            send(x_out.at[at], x_in.at[at], rs_x_s.at[at], rs_x_r.at[at],
                 {"tensor": chip_at(step) * 2 + core})
        )

    def inverse_of(block):
        total = squares[0, pl.ds(block, 1), :]
        for i in range(1, parts):
            total = total + squares[i, pl.ds(block, 1), :]
        return lax.rsqrt(total / (features * parts) + 1e-05)

    span = 2 * rows
    tile = min(features, 512)

    def mask_chip(at):
        for half in range(2):
            block = at * 2 + half
            place = block * rows + lax.broadcasted_iota(jnp.int32, (rows, columns), 0)
            live = (place < length[0]).astype(F32).astype(BF16)
            mask_k[half * rows : (half + 1) * rows, :] = got_k[block] * live
            mask_v[half * rows : (half + 1) * rows, :] = got_v[block] * live

    def gram_add(at, first):
        right_k = jnp.dot(mask_k[...], kr_v[...], preferred_element_type=F32)
        right_v = jnp.dot(mask_v[...], vr_v[...], preferred_element_type=F32)
        for half in range(2):
            block = at * 2 + half
            left = left_t[block] * inverse_of(block)
            for i, right in enumerate((right_k, right_v)):
                term = jnp.dot(
                    left[i * rank : (i + 1) * rank],
                    right[half * rows : (half + 1) * rows],
                    precision=lax.Precision.HIGHEST,
                    preferred_element_type=F32,
                )
                here = slice(i * rank, (i + 1) * rank)
                if first and half == 0:
                    gram_rows[here, :] = term
                else:
                    gram_rows[here, :] += term

    def hid_copy(at):
        to = pl.ds(pl.multiple_of(at * span, span), span)
        return pltpu.make_async_copy(hid_v.at[to], hidden_out.at[to], hid_sem.at[at])

    def back(at):
        to = pl.ds(pl.multiple_of(at * span, span), span)
        contract = (((1,), (1,)), ((), ()))

        def one(i, carry):
            here = pl.ds(pl.multiple_of(i * tile, tile), tile)
            total = lax.dot_general(
                mask_k[...], kw_v[here, :], contract, preferred_element_type=F32
            ) + lax.dot_general(
                mask_v[...], vw_v[here, :], contract, preferred_element_type=F32
            )
            hid_v[to, here] = total.astype(BF16)
            return carry

        lax.fori_loop(0, features // tile, one, 0)
        hid_copy(at).start()

    for copy in own_copies:
        copy.wait()
    for copy in ag_sib:
        copy.wait_recv()
    mask_chip(chip)
    back(chip)
    for copy in sq:
        copy.wait_recv()
    gram_add(chip, True)

    for pair in ag_x:
        for copy in pair:
            copy.wait_send()
    for copy in rs_x:
        copy.start()
    passed = []
    for step in range(1, chips):
        origin = chip_at(-step) * 2 + core
        for i, (_, got) in enumerate(grads):
            ag_x[step - 1][i].wait_recv()
            copy = send(got.at[origin], got.at[origin], ag_f_s.at[step - 1, i],
                        ag_f_r.at[step - 1, i], {"tensor": sibling})
            copy.start()
            passed.append(copy)

    for step in range(1, chips):
        at = chip_at(-step)
        for i in range(2):
            passed[2 * (step - 1) + i].wait_recv()
        mask_chip(at)
        gram_add(at, False)
        if step == chips - 1:
            half = gram_rows.shape[0] // 2
            gram_in[me] = jnp.concatenate(
                [gram_rows[pl.ds(0, half, stride=2), :], gram_rows[pl.ds(1, half, stride=2), :]],
                axis=1,
            )
            gr = [
                send(gram_in.at[me], gram_in.at[me], gr_s.at[to - 1], gr_r.at[to - 1],
                     {"tensor": lax.rem(me + to, parts)})
                for to in range(1, parts)
            ]
            for copy in gr:
                copy.start()
        back(at)

    for copy in gr:
        copy.wait_recv()
    gram = gram_in[0]
    for i in range(1, parts):
        gram = gram + gram_in[i]
    flat_in[doc] = (gram / slots).astype(BF16)

    def flat_copy(step):
        return send(flat_in.at[doc], flat_in.at[doc], fl_s.at[step - 1], fl_r.at[step - 1],
                    {"dp": lax.rem(doc + step, docs)})

    def flat_start(step, carry):
        flat_copy(step).start()
        return carry

    def flat_wait(step, carry):
        flat_copy(step).wait()
        return carry

    lax.fori_loop(1, docs, flat_start, 0)

    last = chips - 1
    rs_sib(last).wait_recv()
    own = partial[2 * last + 1].astype(F32) + sib_in[last].astype(F32)
    inverse = jnp.broadcast_to(inverse_of(me), (LANES, rows)).T

    lax.fori_loop(1, docs, flat_wait, 0)

    def score(i, carry):
        flat = flat_in[i].astype(F32)
        total = jnp.zeros((queries.shape[0], LANES), F32)
        for j in range(flat.shape[0]):
            total = total + queries[:, j * LANES : (j + 1) * LANES].astype(F32) * flat[j : j + 1]
        score_out[i] = total
        return carry

    lax.fori_loop(0, docs, score, 0)

    for copy in rs_x:
        copy.wait_recv()
    for i in range(chips - 1):
        own = own + x_in[i].astype(F32)
    for i in range(columns // LANES):
        here = slice(i * LANES, (i + 1) * LANES)
        there = slice(columns + i * LANES, columns + (i + 1) * LANES)
        key_out[:, here] = (own[:, here] * inverse).astype(BF16)
        value_out[:, here] = (own[:, there] * inverse).astype(BF16)

    for copy in ag_sib + passed + sq + gr + rs_x:
        copy.wait_send()
    for i in range(chips):
        rs_sib(i).wait_send()
        hid_copy(i).wait()


def body(
    residual,
    norm_gain,
    key_weight,
    value_weight,
    key_grad,
    value_grad,
    key_left,
    value_left,
    key_right,
    value_right,
    queries,
    doc_lengths,
):
    parts, docs = lax.axis_size("tensor"), lax.axis_size("dp")
    chips = parts // 2
    slots, features = residual.shape
    rows = slots // parts
    columns, rank = key_weight.shape[1], key_left.shape[1]
    hbm = pl.BlockSpec(memory_space=pl.ANY)
    vmem = pl.BlockSpec(memory_space=pltpu.VMEM)
    dma = pltpu.SemaphoreType.DMA
    flat_rows = 2 * rank * rank // LANES
    key_out, value_out, hidden_grad, shares = pl.pallas_call(
        functools.partial(kernel, parts, docs),
        out_shape=(
            jax.ShapeDtypeStruct((rows, columns), BF16),
            jax.ShapeDtypeStruct((rows, columns), BF16),
            jax.ShapeDtypeStruct((slots, features), BF16),
            jax.ShapeDtypeStruct((docs, queries.shape[0], LANES), F32),
        ),
        in_specs=[hbm] * 10 + [vmem, pl.BlockSpec(memory_space=pltpu.SMEM)],
        out_specs=(vmem, vmem, hbm, vmem),
        scratch_shapes=[
            pltpu.VMEM((slots, features), BF16),
            pltpu.VMEM((1, features), F32),
            pltpu.VMEM((features, columns), BF16),
            pltpu.VMEM((features, columns), BF16),
            pltpu.VMEM((features, rank), BF16),
            pltpu.VMEM((features, rank), BF16),
            pltpu.VMEM((features, 2 * rank), BF16),
            pltpu.VMEM((columns, rank), BF16),
            pltpu.VMEM((columns, rank), BF16),
            pltpu.VMEM((parts, rows, columns), BF16),
            pltpu.VMEM((parts, rows, columns), BF16),
            pltpu.VMEM((2 * rows, columns), BF16),
            pltpu.VMEM((2 * rows, columns), BF16),
            pltpu.VMEM((parts, rows, 2 * columns), BF16),
            pltpu.VMEM((chips, rows, 2 * columns), BF16),
            pltpu.VMEM((chips - 1, rows, 2 * columns), BF16),
            pltpu.VMEM((chips - 1, rows, 2 * columns), BF16),
            pltpu.VMEM((parts, 2 * rank, rows), F32),
            pltpu.VMEM((parts, parts, rows), F32),
            pltpu.VMEM((2 * rank, rank), F32),
            pltpu.VMEM((parts, flat_rows, LANES), F32),
            pltpu.VMEM((docs, flat_rows, LANES), BF16),
            pltpu.VMEM((slots, features), BF16),
            dma((7,)),
            dma((parts,)),
            dma((2,)),
            dma((chips,)),
            dma((2,)),
            dma((2,)),
            dma((chips - 1, 2)),
            dma((chips - 1, 2)),
            dma((chips - 1, 2)),
            dma((chips - 1, 2)),
            dma((chips,)),
            dma((chips,)),
            dma((chips - 1,)),
            dma((chips - 1,)),
            dma((parts - 1,)),
            dma((parts - 1,)),
            dma((parts - 1,)),
            dma((parts - 1,)),
            dma((docs - 1,)),
            dma((docs - 1,)),
        ],
        compiler_params=pltpu.CompilerParams(
            collective_id=0, has_side_effects=True, vmem_limit_bytes=56 * 2**20
        ),
    )(
        residual,
        norm_gain.reshape(1, -1),
        key_weight,
        value_weight,
        key_grad,
        value_grad,
        key_left,
        value_left,
        key_right,
        value_right,
        queries,
        doc_lengths,
    )
    return key_out, value_out, hidden_grad, jnp.sum(shares, axis=2)


def solution(mesh):
    in_specs = (
        P(("groups", "dp"), "tensor"),
        P("tensor"),
        P("tensor", None),
        P("tensor", None),
        P(("groups", "dp", "tensor"), None),
        P(("groups", "dp", "tensor"), None),
        P("tensor", None),
        P("tensor", None),
        P(),
        P(),
        P(("dp", "tensor"), None),
        P(("groups", "dp")),
    )
    out_specs = (
        P(("groups", "dp", "tensor"), None),
        P(("groups", "dp", "tensor"), None),
        P(("groups", "dp"), "tensor"),
        P("groups", ("dp", "tensor")),
    )
    return jax.shard_map(body, mesh=mesh, in_specs=in_specs, out_specs=out_specs, check_vma=False)
```

time: 127 us -> 57.8 us (0.46)
  waiting for transfers between devices: 50.3 us -> 0 us
  Pallas kernels: 0 us -> 39.5 us
  matrix products: 26.5 us -> 0 us
  blocking collectives: 21.9 us -> 0 us
  between operations: 14.7 us -> 1.29 us
  local copies, waits for them, and re-layouts: 2.99 us -> 15.2 us
  other arithmetic: 9.81 us -> 1.36 us
    pallas_call x0 -> x1, Pallas kernels: none -> 39.5 us  [body(): pl.pallas_call(functools.partial(kernel, parts, docs), out_shape=(jax.Sha...]
    dot_general x11 -> x0, matrix products: 26.5 us -> none  [the longest x1 5.37 us: body(): jnp.dot(normed, value_weight, preferred_element_type=jnp.float32)]
    psum x1 -> x0, waiting for transfers between devices: 23.4 us -> none  [body(): lax.psum(value_first.astype(jnp.bfloat16), 'tensor').astype(jnp.float32)]
    all_gather x2 -> x0, waiting for transfers between devices: 17.8 us -> none  [the longest x1 17.7 us: body(): lax.all_gather(key_own, 'tensor', axis=0, tiled=True)]
    all_gather x1 -> x0, blocking collectives: 13.6 us -> none  [body(): every_doc = lax.all_gather(flat[None, :], 'dp', axis=0, tiled=True)]
    unnamed x24 -> x7, local copies, waits for them, and re-layouts: 1.75 us -> 15.2 us
    reduce_scatter x1 -> x0, waiting for transfers between devices: 8.47 us -> none  [body(): lax.psum_scatter(jnp.concatenate(pieces, axis=1).astype(jnp.bfloat16), 't...]
    psum x1 -> x0, blocking collectives: 8.35 us -> none  [body(): square_sum = lax.psum(jnp.sum(widened * widened, axis=1), 'tensor')]
  transfers between devices with their start and end apart: 4 -> 0, of which waited for: 3 -> 0; matrix products, arithmetic and copies ran while one was open for 27% -> 0% of each run, Pallas kernels for 0% -> 0%
where the time goes in v1:
time: 57.8 us; the launch traced here: 57.3 us
  Pallas kernels  39.5 us (68%)
  local copies, waits for them, and re-layouts  15.2 us (26%)
  other arithmetic  1.36 us (2%)
  between operations  1.29 us (2%)
    pallas_call x1, Pallas kernels, body(): pl.pallas_call(functools.partial(kernel, parts, docs), out_shape=(jax.Sha...  39.5 us
    unnamed x7, local copies, waits for them, and re-layouts  15.2 us
    reduce_sum x1, other arithmetic, body(): return (key_out, value_out, hidden_grad, jnp.sum(shares, axis=2))  1.36 us

profile of v1, /device:TPU:0, one launch (start us, length us, event | category | flops | bytes accessed | tf_op | source)
XLA Modules:
  0.0 57.3 jit_solution(16054879250026924149)
XLA Ops:
  1.3 1.6 %copy.18.key_right = bf16[512,64]{1,0:T(8,128)(2,1)} copy(bf16[512,64]{0,1:T(8,128)(2,1)} %param.20) | data formatting | bytes 131072 | tf_op args[8]
  2.9 1.6 %copy.19.value_right = bf16[512,64]{1,0:T(8,128)(2,1)} copy(bf16[512,64]{0,1:T(8,128)(2,1)} %param.21) | data formatting | bytes 131072 | tf_op args[9]
  4.5 2.0 %copy.16.key_left = bf16[2048,64]{1,0:T(8,128)(2,1)} copy(bf16[2048,64]{0,1:T(8,128)(2,1)} %param.18) | data formatting | bytes 524288 | tf_op args[6]
  6.4 2.0 %copy.17.value_left = bf16[2048,64]{1,0:T(8,128)(2,1)} copy(bf16[2048,64]{0,1:T(8,128)(2,1)} %param.19) | data formatting | bytes 524288 | tf_op args[7]
  8.4 39.5 %shard_map.147 = (bf16[256,512]{1,0:T(8,128)(2,1)}, bf16[256,512]{1,0:T(8,128)(2,1)}, bf16[1024,2048]{1,0:T(8,128)(2,1)}, f32[4,4,128]{2,1,0:T(4,128)}) custom-call(bf16[1024,2048]{1,0:T(8,128)(2,1)} %residual.1, f32[1,2048]{1,0:T(1,128)} %bitcast.1, bf16[2048,512]{1,0:T(8,128)(2,1)} %key_weight.1, bf16[2048,512]{1,0:T(8,128)(2,1)} %value_weight.1, ...), custom_call_target="tpu_custom_call" | custom-call | tf_op jit(solution)/shard_map/pallas_call | solution.py:409
  47.9 1.4 %reduce_sum.9 = f32[4,4]{1,0:T(4,128)} reduce(f32[4,4,128]{2,1,0:T(4,128)} %get-tuple-element.11, f32[]{:T(128)} %constant.0.clone.1), dimensions={2}, to_apply=%region_0.0 | reduce | flops 2032 | bytes 8260 | tf_op jit(solution)/shard_map/reduce_sum | solution.py:481
  49.2 1.7 %copy.24 = bf16[256,512]{1,0:T(8,128)(2,1)} copy(bf16[256,512]{1,0:T(8,128)(2,1)} %get-tuple-element.16) | data formatting | bytes 524288
  50.9 1.7 %copy.25 = bf16[256,512]{1,0:T(8,128)(2,1)} copy(bf16[256,512]{1,0:T(8,128)(2,1)} %get-tuple-element.17) | data formatting | bytes 524288
  52.6 4.8 %copy.26 = bf16[1024,2048]{1,0:T(8,128)(2,1)} copy(bf16[1024,2048]{1,0:T(8,128)(2,1)} %get-tuple-element.18) | data formatting | bytes 8388608

commit v2 on v1

--- a/solution.py
+++ b/solution.py
@@ -34,8 +34,6 @@
     gain_v,
     kw_v,
     vw_v,
-    kl_v,
-    vl_v,
     left_w,
     kr_v,
     vr_v,
@@ -52,11 +50,9 @@
     gram_rows,
     gram_in,
     flat_in,
-    hid_v,
     load_sem,
     res_sem,
     own_sem,
-    hid_sem,
     ag_sib_s,
     ag_sib_r,
     ag_x_s,
@@ -78,7 +74,7 @@
     slots, features = res_v.shape
     rows = slots // parts
     columns = kw_v.shape[1]
-    rank = kl_v.shape[1]
+    rank = kr_v.shape[0]
     me = lax.axis_index("tensor")
     doc = lax.axis_index("dp")
     chip, core = me // 2, lax.rem(me, 2)
@@ -102,6 +98,8 @@
         other = lax.rem(order, 2)
         return chip_at(step) * 2 + jnp.where(other == 0, 1 - core, core)
 
+    contract = (((1,), (1,)), ((), ()))
+
     loads = [
         pltpu.make_async_copy(src, dst, load_sem.at[i])
         for i, (src, dst) in enumerate(
@@ -109,8 +107,8 @@
                 (gain, gain_v),
                 (key_weight, kw_v),
                 (value_weight, vw_v),
-                (key_left, kl_v),
-                (value_left, vl_v),
+                (key_left, left_w.at[:rank]),
+                (value_left, left_w.at[rank:]),
                 (key_right, kr_v),
                 (value_right, vr_v),
             )
@@ -172,8 +170,6 @@
 
     for copy in loads:
         copy.wait()
-    left_w[:, :rank] = kl_v[...]
-    left_w[:, rank:] = vl_v[...]
 
     def rs_sib(at):
         return send(partial.at[2 * at], sib_in.at[at], rs_sib_s.at[at], rs_sib_r.at[at],
@@ -195,7 +191,9 @@
         partial[order, :, columns:] = jnp.dot(
             scaled, vw_v[...], preferred_element_type=F32
         ).astype(BF16)
-        left_t[block] = jnp.dot(scaled, left_w[...], preferred_element_type=F32).T
+        left_t[block] = lax.dot_general(
+            left_w[...], scaled, contract, preferred_element_type=F32
+        )
 
         @pl.when(lax.rem(order, 2) == 0)
         def _():
@@ -243,8 +241,12 @@
             mask_v[half * rows : (half + 1) * rows, :] = got_v[block] * live
 
     def gram_add(at, first):
-        right_k = jnp.dot(mask_k[...], kr_v[...], preferred_element_type=F32)
-        right_v = jnp.dot(mask_v[...], vr_v[...], preferred_element_type=F32)
+        right_k = lax.dot_general(
+            mask_k[...], kr_v[...], contract, preferred_element_type=F32
+        )
+        right_v = lax.dot_general(
+            mask_v[...], vr_v[...], contract, preferred_element_type=F32
+        )
         for half in range(2):
             block = at * 2 + half
             left = left_t[block] * inverse_of(block)
@@ -261,13 +263,8 @@
                 else:
                     gram_rows[here, :] += term
 
-    def hid_copy(at):
-        to = pl.ds(pl.multiple_of(at * span, span), span)
-        return pltpu.make_async_copy(hid_v.at[to], hidden_out.at[to], hid_sem.at[at])
-
     def back(at):
         to = pl.ds(pl.multiple_of(at * span, span), span)
-        contract = (((1,), (1,)), ((), ()))
 
         def one(i, carry):
             here = pl.ds(pl.multiple_of(i * tile, tile), tile)
@@ -276,11 +273,10 @@
             ) + lax.dot_general(
                 mask_v[...], vw_v[here, :], contract, preferred_element_type=F32
             )
-            hid_v[to, here] = total.astype(BF16)
+            hidden_out[to, here] = total.astype(BF16)
             return carry
 
         lax.fori_loop(0, features // tile, one, 0)
-        hid_copy(at).start()
 
     for copy in own_copies:
         copy.wait()
@@ -380,7 +376,20 @@
         copy.wait_send()
     for i in range(chips):
         rs_sib(i).wait_send()
-        hid_copy(i).wait()
+
+
+def finish(key_in, value_in, hidden_in, shares, key_out, value_out, hidden_out, scores, sem):
+    copies = [
+        pltpu.make_async_copy(src, dst, sem.at[i])
+        for i, (src, dst) in enumerate(
+            ((hidden_in, hidden_out), (key_in, key_out), (value_in, value_out))
+        )
+    ]
+    for copy in copies:
+        copy.start()
+    scores[...] = jnp.sum(shares[...], axis=2)
+    for copy in copies:
+        copy.wait()
 
 
 def body(
@@ -409,23 +418,21 @@
     key_out, value_out, hidden_grad, shares = pl.pallas_call(
         functools.partial(kernel, parts, docs),
         out_shape=(
-            jax.ShapeDtypeStruct((rows, columns), BF16),
-            jax.ShapeDtypeStruct((rows, columns), BF16),
-            jax.ShapeDtypeStruct((slots, features), BF16),
-            jax.ShapeDtypeStruct((docs, queries.shape[0], LANES), F32),
+            pltpu.VMEM((rows, columns), BF16),
+            pltpu.VMEM((rows, columns), BF16),
+            pltpu.VMEM((slots, features), BF16),
+            pltpu.VMEM((docs, queries.shape[0], LANES), F32),
         ),
         in_specs=[hbm] * 10 + [vmem, pl.BlockSpec(memory_space=pltpu.SMEM)],
-        out_specs=(vmem, vmem, hbm, vmem),
+        out_specs=(vmem,) * 4,
         scratch_shapes=[
             pltpu.VMEM((slots, features), BF16),
             pltpu.VMEM((1, features), F32),
             pltpu.VMEM((features, columns), BF16),
             pltpu.VMEM((features, columns), BF16),
-            pltpu.VMEM((features, rank), BF16),
-            pltpu.VMEM((features, rank), BF16),
-            pltpu.VMEM((features, 2 * rank), BF16),
-            pltpu.VMEM((columns, rank), BF16),
-            pltpu.VMEM((columns, rank), BF16),
+            pltpu.VMEM((2 * rank, features), BF16),
+            pltpu.VMEM((rank, columns), BF16),
+            pltpu.VMEM((rank, columns), BF16),
             pltpu.VMEM((parts, rows, columns), BF16),
             pltpu.VMEM((parts, rows, columns), BF16),
             pltpu.VMEM((2 * rows, columns), BF16),
@@ -439,11 +446,9 @@
             pltpu.VMEM((2 * rank, rank), F32),
             pltpu.VMEM((parts, flat_rows, LANES), F32),
             pltpu.VMEM((docs, flat_rows, LANES), BF16),
-            pltpu.VMEM((slots, features), BF16),
             dma((7,)),
             dma((parts,)),
             dma((2,)),
-            dma((chips,)),
             dma((2,)),
             dma((2,)),
             dma((chips - 1, 2)),
@@ -462,7 +467,7 @@
             dma((docs - 1,)),
         ],
         compiler_params=pltpu.CompilerParams(
-            collective_id=0, has_side_effects=True, vmem_limit_bytes=56 * 2**20
+            collective_id=0, has_side_effects=True, vmem_limit_bytes=58 * 2**20
         ),
     )(
         residual,
@@ -471,14 +476,26 @@
         value_weight,
         key_grad,
         value_grad,
-        key_left,
-        value_left,
-        key_right,
-        value_right,
+        key_left.T,
+        value_left.T,
+        key_right.T,
+        value_right.T,
         queries,
         doc_lengths,
     )
-    return key_out, value_out, hidden_grad, jnp.sum(shares, axis=2)
+    return pl.pallas_call(
+        finish,
+        out_shape=(
+            jax.ShapeDtypeStruct((rows, columns), BF16),
+            jax.ShapeDtypeStruct((rows, columns), BF16),
+            jax.ShapeDtypeStruct((slots, features), BF16),
+            jax.ShapeDtypeStruct((docs, queries.shape[0]), F32),
+        ),
+        in_specs=[vmem] * 4,
+        out_specs=(hbm, hbm, hbm, vmem),
+        scratch_shapes=[dma((3,))],
+        compiler_params=pltpu.CompilerParams(vmem_limit_bytes=2 * 2**20),
+    )(key_out, value_out, hidden_grad, shares)
 
 
 def solution(mesh):

time: 57.8 us -> 42.9 us (0.74)
  local copies, waits for them, and re-layouts: 15.2 us -> 0 us
  Pallas kernels: 39.5 us -> 41.4 us
  other arithmetic: 1.36 us -> 0 us
    unnamed x7 -> x0, local copies, waits for them, and re-layouts: 15.2 us -> none
    pallas_call x1 -> x2, Pallas kernels: 39.5 us -> 41.4 us  [the longest x1 38.6 us: body(): pl.pallas_call(functools.partial(kernel, parts, docs), out_shape=(pltpu.V...]
    reduce_sum x1 -> x0, other arithmetic: 1.36 us -> none  [body(): return (key_out, value_out, hidden_grad, jnp.sum(shares, axis=2))]
where the time goes in v2:
time: 42.9 us; the launch traced here: 42.7 us
  Pallas kernels  41.4 us (97%)
  between operations  1.29 us (3%)
    pallas_call x1, Pallas kernels, body(): pl.pallas_call(functools.partial(kernel, parts, docs), out_shape=(pltpu.V...  38.6 us
    pallas_call x1, Pallas kernels, body(): pl.pallas_call(finish, out_shape=(jax.ShapeDtypeStruct((rows, columns), B...  2.77 us

profile of v2, /device:TPU:0, one launch (start us, length us, event | category | flops | bytes accessed | tf_op | source)
XLA Modules:
  0.0 42.7 jit_solution(983419937193007075)
XLA Ops:
  1.3 38.6 %shard_map.147 = (bf16[256,512]{1,0:T(8,128)(2,1)S(1)}, bf16[256,512]{1,0:T(8,128)(2,1)S(1)}, bf16[1024,2048]{1,0:T(8,128)(2,1)S(1)}, f32[4,4,128]{2,1,0:T(4,128)S(1)}) custom-call(bf16[1024,2048]{1,0:T(8,128)(2,1)} %residual.1, f32[1,2048]{1,0:T(1,128)} %bitcast.9, bf16[2048,512]{1,0:T(8,128)(2,1)} %key_weight.1, bf16[2048,512]{1,0:T(8,128)(2,1)} %value_weight.1, ...), custom_call_target="tpu_custom_call" | custom-call | tf_op jit(solution)/shard_map/pallas_call | solution.py:418
  39.9 2.8 %shard_map.148 = (bf16[256,512]{1,0:T(8,128)(2,1)}, bf16[256,512]{1,0:T(8,128)(2,1)}, bf16[1024,2048]{1,0:T(8,128)(2,1)}, f32[4,4]{1,0:T(4,128)}) custom-call(bf16[256,512]{1,0:T(8,128)(2,1)S(1)} %get-tuple-element.8.key_in, bf16[256,512]{1,0:T(8,128)(2,1)S(1)} %get-tuple-element.9.value_in, bf16[1024,2048]{1,0:T(8,128)(2,1)S(1)} %get-tuple-element.10.hidden_in, ...), custom_call_target="tpu_custom_call" | custom-call | tf_op jit(solution)/shard_map/pallas_call | solution.py:486

commit v3 on v2

--- a/solution.py
+++ b/solution.py
@@ -9,6 +9,8 @@
 
 F32, BF16 = jnp.float32, jnp.bfloat16
 LANES = 128
+PIECES = 4
+SPLIT = 8
 
 
 def kernel(
@@ -211,6 +213,8 @@
     for copy in sq:
         copy.start()
 
+    size = rows // PIECES
+    pieces = [slice(i * size, (i + 1) * size) for i in range(PIECES)]
     rs_x = []
     for step in range(1, chips):
         at = step - 1
@@ -219,8 +223,11 @@
             partial[2 * at + 1].astype(F32) + sib_in[at].astype(F32)
         ).astype(BF16)
         rs_x.append(
-            send(x_out.at[at], x_in.at[at], rs_x_s.at[at], rs_x_r.at[at],
-                 {"tensor": chip_at(step) * 2 + core})
+            [
+                send(x_out.at[at, here], x_in.at[at, here], rs_x_s.at[at, i], rs_x_r.at[at, i],
+                     {"tensor": chip_at(step) * 2 + core})
+                for i, here in enumerate(pieces)
+            ]
         )
 
     def inverse_of(block):
@@ -291,8 +298,8 @@
     for pair in ag_x:
         for copy in pair:
             copy.wait_send()
-    for copy in rs_x:
-        copy.start()
+    for group in rs_x:
+        group[0].start()
     passed = []
     for step in range(1, chips):
         origin = chip_at(-step) * 2 + core
@@ -307,6 +314,9 @@
         at = chip_at(-step)
         for i in range(2):
             passed[2 * (step - 1) + i].wait_recv()
+        if step == chips - 1:
+            for group in rs_x:
+                group[1].start()
         mask_chip(at)
         gram_add(at, False)
         if step == chips - 1:
@@ -322,6 +332,9 @@
             ]
             for copy in gr:
                 copy.start()
+            for i in range(2, PIECES):
+                for group in rs_x:
+                    group[i].start()
         back(at)
 
     for copy in gr:
@@ -347,7 +360,6 @@
 
     last = chips - 1
     rs_sib(last).wait_recv()
-    own = partial[2 * last + 1].astype(F32) + sib_in[last].astype(F32)
     inverse = jnp.broadcast_to(inverse_of(me), (LANES, rows)).T
 
     lax.fori_loop(1, docs, flat_wait, 0)
@@ -362,28 +374,32 @@
 
     lax.fori_loop(0, docs, score, 0)
 
-    for copy in rs_x:
-        copy.wait_recv()
-    for i in range(chips - 1):
-        own = own + x_in[i].astype(F32)
-    for i in range(columns // LANES):
-        here = slice(i * LANES, (i + 1) * LANES)
-        there = slice(columns + i * LANES, columns + (i + 1) * LANES)
-        key_out[:, here] = (own[:, here] * inverse).astype(BF16)
-        value_out[:, here] = (own[:, there] * inverse).astype(BF16)
-
-    for copy in ag_sib + passed + sq + gr + rs_x:
+    for at, piece in enumerate(pieces):
+        for group in rs_x:
+            group[at].wait_recv()
+        own = partial[2 * last + 1, piece].astype(F32) + sib_in[last, piece].astype(F32)
+        for i in range(chips - 1):
+            own = own + x_in[i, piece].astype(F32)
+        scale = inverse[piece]
+        for i in range(columns // LANES):
+            here = slice(i * LANES, (i + 1) * LANES)
+            there = slice(columns + i * LANES, columns + (i + 1) * LANES)
+            key_out[piece, here] = (own[:, here] * scale).astype(BF16)
+            value_out[piece, here] = (own[:, there] * scale).astype(BF16)
+
+    for copy in ag_sib + passed + sq + gr + [copy for group in rs_x for copy in group]:
         copy.wait_send()
     for i in range(chips):
         rs_sib(i).wait_send()
 
 
 def finish(key_in, value_in, hidden_in, shares, key_out, value_out, hidden_out, scores, sem):
+    size = hidden_in.shape[0] // SPLIT
+    views = [slice(i * size, (i + 1) * size) for i in range(SPLIT)]
+    pairs = [(hidden_in.at[here], hidden_out.at[here]) for here in views]
+    pairs += [(key_in, key_out), (value_in, value_out)]
     copies = [
-        pltpu.make_async_copy(src, dst, sem.at[i])
-        for i, (src, dst) in enumerate(
-            ((hidden_in, hidden_out), (key_in, key_out), (value_in, value_out))
-        )
+        pltpu.make_async_copy(src, dst, sem.at[i]) for i, (src, dst) in enumerate(pairs)
     ]
     for copy in copies:
         copy.start()
@@ -457,8 +473,8 @@
             dma((chips - 1, 2)),
             dma((chips,)),
             dma((chips,)),
-            dma((chips - 1,)),
-            dma((chips - 1,)),
+            dma((chips - 1, PIECES)),
+            dma((chips - 1, PIECES)),
             dma((parts - 1,)),
             dma((parts - 1,)),
             dma((parts - 1,)),
@@ -493,7 +509,7 @@
         ),
         in_specs=[vmem] * 4,
         out_specs=(hbm, hbm, hbm, vmem),
-        scratch_shapes=[dma((3,))],
+        scratch_shapes=[dma((SPLIT + 2,))],
         compiler_params=pltpu.CompilerParams(vmem_limit_bytes=2 * 2**20),
     )(key_out, value_out, hidden_grad, shares)
 

time: 42.9 us -> 39.1 us (0.911)
  Pallas kernels: 41.4 us -> 37.7 us
    pallas_call x1, Pallas kernels: 38.6 us -> 34.8 us  [body(): pl.pallas_call(functools.partial(kernel, parts, docs), out_shape=(pltpu.V...]
where the time goes in v3:
time: 39.1 us; the launch traced here: 39 us
  Pallas kernels  37.7 us (96%)
  between operations  1.29 us (3%)
    pallas_call x1, Pallas kernels, body(): pl.pallas_call(functools.partial(kernel, parts, docs), out_shape=(pltpu.V...  34.8 us
    pallas_call x1, Pallas kernels, body(): pl.pallas_call(finish, out_shape=(jax.ShapeDtypeStruct((rows, columns), B...  2.83 us

profile of v3, /device:TPU:0, one launch (start us, length us, event | category | flops | bytes accessed | tf_op | source)
XLA Modules:
  0.0 39.0 jit_solution(1380388846218925243)
XLA Ops:
  1.3 34.8 %shard_map.147 = (bf16[256,512]{1,0:T(8,128)(2,1)S(1)}, bf16[256,512]{1,0:T(8,128)(2,1)S(1)}, bf16[1024,2048]{1,0:T(8,128)(2,1)S(1)}, f32[4,4,128]{2,1,0:T(4,128)S(1)}) custom-call(bf16[1024,2048]{1,0:T(8,128)(2,1)} %residual.1, f32[1,2048]{1,0:T(1,128)} %bitcast.9, bf16[2048,512]{1,0:T(8,128)(2,1)} %key_weight.1, bf16[2048,512]{1,0:T(8,128)(2,1)} %value_weight.1, ...), custom_call_target="tpu_custom_call" | custom-call | tf_op jit(solution)/shard_map/pallas_call | solution.py:434
  36.1 2.8 %shard_map.148 = (bf16[256,512]{1,0:T(8,128)(2,1)}, bf16[256,512]{1,0:T(8,128)(2,1)}, bf16[1024,2048]{1,0:T(8,128)(2,1)}, f32[4,4]{1,0:T(4,128)}) custom-call(bf16[256,512]{1,0:T(8,128)(2,1)S(1)} %get-tuple-element.8.key_in, bf16[256,512]{1,0:T(8,128)(2,1)S(1)} %get-tuple-element.9.value_in, bf16[1024,2048]{1,0:T(8,128)(2,1)S(1)} %get-tuple-element.10.hidden_in, ...), custom_call_target="tpu_custom_call" | custom-call | tf_op jit(solution)/shard_map/pallas_call | solution.py:502

commit v4 on v3

--- a/solution.py
+++ b/solution.py
@@ -48,6 +48,7 @@
     x_out,
     x_in,
     left_t,
+    right_g,
     squares,
     gram_rows,
     gram_in,
@@ -71,6 +72,8 @@
     gr_r,
     fl_s,
     fl_r,
+    rt_s,
+    rt_r,
 ):
     chips = parts // 2
     slots, features = res_v.shape
@@ -141,14 +144,23 @@
         return carry
 
     lax.fori_loop(1, docs, greet, 0)
-    for copy in loads[:5]:
-        copy.start()
     for order in range(parts):
         res_copy(order).start()
-    for copy in loads[5:]:
+    for copy in own_copies + loads[5:] + loads[:5]:
         copy.start()
-    for copy in own_copies:
-        copy.start()
+
+    def square(order, carry):
+        res_copy(order).wait()
+        block = block_of(order)
+        wide = res_v[pl.ds(pl.multiple_of(block * rows, rows), rows), :].astype(F32)
+        squared = wide * wide
+        lane_sum = squared[:, :LANES]
+        for i in range(1, features // LANES):
+            lane_sum = lane_sum + squared[:, i * LANES : (i + 1) * LANES]
+        squares[me, pl.ds(block, 1), :] = jnp.sum(lane_sum.T, axis=0, keepdims=True)
+        return carry
+
+    lax.fori_loop(0, parts, square, 0)
     pl.semaphore_wait(barrier, parts - 1 + docs - 1)
 
     grads = ((key_grad, got_k), (value_grad, got_v))
@@ -164,13 +176,43 @@
         send(src, got.at[me], ag_sib_s.at[i], ag_sib_r.at[i], {"tensor": sibling})
         for i, (src, got) in enumerate(grads)
     ]
+    sq = [
+        send(squares.at[me], squares.at[me], sq_s.at[step - 1], sq_r.at[step - 1],
+             {"tensor": lax.rem(me + step, parts)})
+        for step in range(1, parts)
+    ]
     for pair in ag_x:
-        for copy in pair:
-            copy.start()
+        pair[0].start()
+    for copy in sq:
+        copy.start()
+    for copy in own_copies + loads[5:]:
+        copy.wait()
+
+    def masked(block, got):
+        place = block * rows + lax.broadcasted_iota(jnp.int32, (rows, columns), 0)
+        return got[block] * (place < length[0]).astype(F32).astype(BF16)
+
+    for i, (got, right) in enumerate(((got_k, kr_v), (got_v, vr_v))):
+        right_g[me, :, i * rank : (i + 1) * rank] = lax.dot_general(
+            masked(me, got), right[...], contract, preferred_element_type=F32
+        ).astype(BF16)
+    def right_send(block, at, target):
+        return send(right_g.at[block], right_g.at[block], rt_s.at[at], rt_r.at[at],
+                    {"tensor": target})
+
+    rt_x = [
+        right_send(me, step - 1, chip_at(step) * 2 + core) for step in range(1, chips)
+    ]
+    rt_sib = right_send(me, chips - 1, sibling)
+    for copy in rt_x + [rt_sib]:
+        copy.start()
+
+    for pair in ag_x:
+        pair[1].start()
     for copy in ag_sib:
         copy.start()
 
-    for copy in loads:
+    for copy in loads[:5]:
         copy.wait()
 
     def rs_sib(at):
@@ -178,15 +220,9 @@
                     {"tensor": sibling})
 
     def forward(order, carry):
-        res_copy(order).wait()
         block = block_of(order)
         wide = res_v[pl.ds(pl.multiple_of(block * rows, rows), rows), :].astype(F32)
         scaled = (wide * gain_v[...]).astype(BF16)
-        squared = wide * wide
-        lane_sum = squared[:, :LANES]
-        for i in range(1, features // LANES):
-            lane_sum = lane_sum + squared[:, i * LANES : (i + 1) * LANES]
-        squares[me, pl.ds(block, 1), :] = jnp.sum(lane_sum.T, axis=0, keepdims=True)
         partial[order, :, :columns] = jnp.dot(
             scaled, kw_v[...], preferred_element_type=F32
         ).astype(BF16)
@@ -205,13 +241,12 @@
 
     lax.fori_loop(0, parts, forward, 0)
 
-    sq = [
-        send(squares.at[me], squares.at[me], sq_s.at[step - 1], sq_r.at[step - 1],
-             {"tensor": lax.rem(me + step, parts)})
-        for step in range(1, parts)
-    ]
-    for copy in sq:
-        copy.start()
+    rt_pass = []
+    for step in range(1, chips):
+        rt_x[step - 1].wait_recv()
+        origin = chip_at(-step) * 2 + core
+        rt_pass.append(right_send(origin, chips - 1 + step, sibling))
+        rt_pass[-1].start()
 
     size = rows // PIECES
     pieces = [slice(i * size, (i + 1) * size) for i in range(PIECES)]
@@ -242,33 +277,27 @@
     def mask_chip(at):
         for half in range(2):
             block = at * 2 + half
-            place = block * rows + lax.broadcasted_iota(jnp.int32, (rows, columns), 0)
-            live = (place < length[0]).astype(F32).astype(BF16)
-            mask_k[half * rows : (half + 1) * rows, :] = got_k[block] * live
-            mask_v[half * rows : (half + 1) * rows, :] = got_v[block] * live
-
-    def gram_add(at, first):
-        right_k = lax.dot_general(
-            mask_k[...], kr_v[...], contract, preferred_element_type=F32
-        )
-        right_v = lax.dot_general(
-            mask_v[...], vr_v[...], contract, preferred_element_type=F32
-        )
-        for half in range(2):
-            block = at * 2 + half
+            mask_k[half * rows : (half + 1) * rows, :] = masked(block, got_k)
+            mask_v[half * rows : (half + 1) * rows, :] = masked(block, got_v)
+
+    def gram_share():
+        def add(block, total):
             left = left_t[block] * inverse_of(block)
-            for i, right in enumerate((right_k, right_v)):
-                term = jnp.dot(
+            right = right_g[block].astype(F32)
+            return tuple(
+                was
+                + jnp.dot(
                     left[i * rank : (i + 1) * rank],
-                    right[half * rows : (half + 1) * rows],
+                    right[:, i * rank : (i + 1) * rank],
                     precision=lax.Precision.HIGHEST,
                     preferred_element_type=F32,
                 )
-                here = slice(i * rank, (i + 1) * rank)
-                if first and half == 0:
-                    gram_rows[here, :] = term
-                else:
-                    gram_rows[here, :] += term
+                for i, was in enumerate(total)
+            )
+
+        zero = jnp.zeros((rank, rank), F32)
+        for i, share in enumerate(lax.fori_loop(0, parts, add, (zero, zero))):
+            gram_rows[i * rank : (i + 1) * rank, :] = share
 
     def back(at):
         to = pl.ds(pl.multiple_of(at * span, span), span)
@@ -285,21 +314,31 @@
 
         lax.fori_loop(0, features // tile, one, 0)
 
-    for copy in own_copies:
-        copy.wait()
+    for copy in sq + [rt_sib] + rt_pass:
+        copy.wait_recv()
+    gram_share()
+    half = gram_rows.shape[0] // 2
+    gram_in[me] = jnp.concatenate(
+        [gram_rows[pl.ds(0, half, stride=2), :], gram_rows[pl.ds(1, half, stride=2), :]],
+        axis=1,
+    ).astype(BF16)
+    gr = [
+        send(gram_in.at[me], gram_in.at[me], gr_s.at[to - 1], gr_r.at[to - 1],
+             {"tensor": lax.rem(me + to, parts)})
+        for to in range(1, parts)
+    ]
+    for copy in gr:
+        copy.start()
+
+    for i in range(PIECES):
+        for group in rs_x:
+            group[i].start()
+
     for copy in ag_sib:
         copy.wait_recv()
     mask_chip(chip)
     back(chip)
-    for copy in sq:
-        copy.wait_recv()
-    gram_add(chip, True)
-
-    for pair in ag_x:
-        for copy in pair:
-            copy.wait_send()
-    for group in rs_x:
-        group[0].start()
+
     passed = []
     for step in range(1, chips):
         origin = chip_at(-step) * 2 + core
@@ -310,38 +349,11 @@
             copy.start()
             passed.append(copy)
 
-    for step in range(1, chips):
-        at = chip_at(-step)
-        for i in range(2):
-            passed[2 * (step - 1) + i].wait_recv()
-        if step == chips - 1:
-            for group in rs_x:
-                group[1].start()
-        mask_chip(at)
-        gram_add(at, False)
-        if step == chips - 1:
-            half = gram_rows.shape[0] // 2
-            gram_in[me] = jnp.concatenate(
-                [gram_rows[pl.ds(0, half, stride=2), :], gram_rows[pl.ds(1, half, stride=2), :]],
-                axis=1,
-            )
-            gr = [
-                send(gram_in.at[me], gram_in.at[me], gr_s.at[to - 1], gr_r.at[to - 1],
-                     {"tensor": lax.rem(me + to, parts)})
-                for to in range(1, parts)
-            ]
-            for copy in gr:
-                copy.start()
-            for i in range(2, PIECES):
-                for group in rs_x:
-                    group[i].start()
-        back(at)
-
     for copy in gr:
         copy.wait_recv()
-    gram = gram_in[0]
+    gram = gram_in[0].astype(F32)
     for i in range(1, parts):
-        gram = gram + gram_in[i]
+        gram = gram + gram_in[i].astype(F32)
     flat_in[doc] = (gram / slots).astype(BF16)
 
     def flat_copy(step):
@@ -357,6 +369,12 @@
         return carry
 
     lax.fori_loop(1, docs, flat_start, 0)
+
+    for step in range(1, chips):
+        for i in range(2):
+            passed[2 * (step - 1) + i].wait_recv()
+        mask_chip(chip_at(-step))
+        back(chip_at(-step))
 
     last = chips - 1
     rs_sib(last).wait_recv()
@@ -387,7 +405,7 @@
             key_out[piece, here] = (own[:, here] * scale).astype(BF16)
             value_out[piece, here] = (own[:, there] * scale).astype(BF16)
 
-    for copy in ag_sib + passed + sq + gr + [copy for group in rs_x for copy in group]:
+    for copy in rt_x + [rt_sib] + rt_pass + ag_sib + [copy for pair in ag_x for copy in pair] + passed + sq + gr + [copy for group in rs_x for copy in group]:
         copy.wait_send()
     for i in range(chips):
         rs_sib(i).wait_send()
@@ -458,9 +476,10 @@
             pltpu.VMEM((chips - 1, rows, 2 * columns), BF16),
             pltpu.VMEM((chips - 1, rows, 2 * columns), BF16),
             pltpu.VMEM((parts, 2 * rank, rows), F32),
+            pltpu.VMEM((parts, rows, 2 * rank), BF16),
             pltpu.VMEM((parts, parts, rows), F32),
             pltpu.VMEM((2 * rank, rank), F32),
-            pltpu.VMEM((parts, flat_rows, LANES), F32),
+            pltpu.VMEM((parts, flat_rows, LANES), BF16),
             pltpu.VMEM((docs, flat_rows, LANES), BF16),
             dma((7,)),
             dma((parts,)),
@@ -481,6 +500,8 @@
             dma((parts - 1,)),
             dma((docs - 1,)),
             dma((docs - 1,)),
+            dma((2 * chips - 1,)),
+            dma((2 * chips - 1,)),
         ],
         compiler_params=pltpu.CompilerParams(
             collective_id=0, has_side_effects=True, vmem_limit_bytes=58 * 2**20

time: 39.1 us -> 38.2 us (0.977)
  Pallas kernels: 37.7 us -> 36.8 us
    pallas_call x1, Pallas kernels: 34.8 us -> 33.9 us  [body(): pl.pallas_call(functools.partial(kernel, parts, docs), out_shape=(pltpu.V...]
where the time goes in v4:
time: 38.2 us; the launch traced here: 38.1 us
  Pallas kernels  36.8 us (96%)
  between operations  1.29 us (3%)
    pallas_call x1, Pallas kernels, body(): pl.pallas_call(functools.partial(kernel, parts, docs), out_shape=(pltpu.V...  33.9 us
    pallas_call x1, Pallas kernels, body(): pl.pallas_call(finish, out_shape=(jax.ShapeDtypeStruct((rows, columns), B...  2.83 us

profile of v4, /device:TPU:0, one launch (start us, length us, event | category | flops | bytes accessed | tf_op | source)
XLA Modules:
  0.0 38.1 jit_solution(12575693947277824496)
XLA Ops:
  1.3 33.9 %shard_map.147 = (bf16[256,512]{1,0:T(8,128)(2,1)S(1)}, bf16[256,512]{1,0:T(8,128)(2,1)S(1)}, bf16[1024,2048]{1,0:T(8,128)(2,1)S(1)}, f32[4,4,128]{2,1,0:T(4,128)S(1)}) custom-call(bf16[1024,2048]{1,0:T(8,128)(2,1)} %residual.1, f32[1,2048]{1,0:T(1,128)} %bitcast.9, bf16[2048,512]{1,0:T(8,128)(2,1)} %key_weight.1, bf16[2048,512]{1,0:T(8,128)(2,1)} %value_weight.1, ...), custom_call_target="tpu_custom_call" | custom-call | tf_op jit(solution)/shard_map/pallas_call | solution.py:452
  35.2 2.8 %shard_map.148 = (bf16[256,512]{1,0:T(8,128)(2,1)}, bf16[256,512]{1,0:T(8,128)(2,1)}, bf16[1024,2048]{1,0:T(8,128)(2,1)}, f32[4,4]{1,0:T(4,128)}) custom-call(bf16[256,512]{1,0:T(8,128)(2,1)S(1)} %get-tuple-element.8.key_in, bf16[256,512]{1,0:T(8,128)(2,1)S(1)} %get-tuple-element.9.value_in, bf16[1024,2048]{1,0:T(8,128)(2,1)S(1)} %get-tuple-element.10.hidden_in, ...), custom_call_target="tpu_custom_call" | custom-call | tf_op jit(solution)/shard_map/pallas_call | solution.py:523

commit v5 on v4

--- a/solution.py
+++ b/solution.py
@@ -149,6 +149,51 @@
     for copy in own_copies + loads[5:] + loads[:5]:
         copy.start()
 
+    pl.semaphore_wait(barrier, parts - 1 + docs - 1)
+
+    grads = ((key_grad, got_k), (value_grad, got_v))
+    ag_x = [
+        [
+            send(src, got.at[me], ag_x_s.at[step - 1, i], ag_x_r.at[step - 1, i],
+                 {"tensor": chip_at(step) * 2 + core})
+            for i, (src, got) in enumerate(grads)
+        ]
+        for step in range(1, chips)
+    ]
+    ag_sib = [
+        send(src, got.at[me], ag_sib_s.at[i], ag_sib_r.at[i], {"tensor": sibling})
+        for i, (src, got) in enumerate(grads)
+    ]
+    sq = [
+        send(squares.at[me], squares.at[me], sq_s.at[step - 1], sq_r.at[step - 1],
+             {"tensor": lax.rem(me + step, parts)})
+        for step in range(1, parts)
+    ]
+    for pair in ag_x:
+        pair[0].start()
+
+    for copy in own_copies + loads[5:]:
+        copy.wait()
+
+    def masked(block, got):
+        place = block * rows + lax.broadcasted_iota(jnp.int32, (rows, columns), 0)
+        return got[block] * (place < length[0]).astype(F32).astype(BF16)
+
+    for i, (got, right) in enumerate(((got_k, kr_v), (got_v, vr_v))):
+        right_g[me, :, i * rank : (i + 1) * rank] = lax.dot_general(
+            masked(me, got), right[...], contract, preferred_element_type=F32
+        ).astype(BF16)
+    def right_send(block, at, target):
+        return send(right_g.at[block], right_g.at[block], rt_s.at[at], rt_r.at[at],
+                    {"tensor": target})
+
+    rt_x = [
+        right_send(me, step - 1, chip_at(step) * 2 + core) for step in range(1, chips)
+    ]
+    rt_sib = right_send(me, chips - 1, sibling)
+    for copy in rt_x + [rt_sib]:
+        copy.start()
+
     def square(order, carry):
         res_copy(order).wait()
         block = block_of(order)
@@ -161,52 +206,8 @@
         return carry
 
     lax.fori_loop(0, parts, square, 0)
-    pl.semaphore_wait(barrier, parts - 1 + docs - 1)
-
-    grads = ((key_grad, got_k), (value_grad, got_v))
-    ag_x = [
-        [
-            send(src, got.at[me], ag_x_s.at[step - 1, i], ag_x_r.at[step - 1, i],
-                 {"tensor": chip_at(step) * 2 + core})
-            for i, (src, got) in enumerate(grads)
-        ]
-        for step in range(1, chips)
-    ]
-    ag_sib = [
-        send(src, got.at[me], ag_sib_s.at[i], ag_sib_r.at[i], {"tensor": sibling})
-        for i, (src, got) in enumerate(grads)
-    ]
-    sq = [
-        send(squares.at[me], squares.at[me], sq_s.at[step - 1], sq_r.at[step - 1],
-             {"tensor": lax.rem(me + step, parts)})
-        for step in range(1, parts)
-    ]
-    for pair in ag_x:
-        pair[0].start()
     for copy in sq:
         copy.start()
-    for copy in own_copies + loads[5:]:
-        copy.wait()
-
-    def masked(block, got):
-        place = block * rows + lax.broadcasted_iota(jnp.int32, (rows, columns), 0)
-        return got[block] * (place < length[0]).astype(F32).astype(BF16)
-
-    for i, (got, right) in enumerate(((got_k, kr_v), (got_v, vr_v))):
-        right_g[me, :, i * rank : (i + 1) * rank] = lax.dot_general(
-            masked(me, got), right[...], contract, preferred_element_type=F32
-        ).astype(BF16)
-    def right_send(block, at, target):
-        return send(right_g.at[block], right_g.at[block], rt_s.at[at], rt_r.at[at],
-                    {"tensor": target})
-
-    rt_x = [
-        right_send(me, step - 1, chip_at(step) * 2 + core) for step in range(1, chips)
-    ]
-    rt_sib = right_send(me, chips - 1, sibling)
-    for copy in rt_x + [rt_sib]:
-        copy.start()
-
     for pair in ag_x:
         pair[1].start()
     for copy in ag_sib:

time: 38.2 us -> 37.7 us (0.987)
  Pallas kernels: 36.8 us -> 36.2 us
    pallas_call x1, Pallas kernels: 33.9 us -> 33.4 us  [body(): pl.pallas_call(functools.partial(kernel, parts, docs), out_shape=(pltpu.V...]
where the time goes in v5:
time: 37.7 us; the launch traced here: 37.5 us
  Pallas kernels  36.2 us (96%)
  between operations  1.29 us (3%)
    pallas_call x1, Pallas kernels, body(): pl.pallas_call(functools.partial(kernel, parts, docs), out_shape=(pltpu.V...  33.4 us
    pallas_call x1, Pallas kernels, body(): pl.pallas_call(finish, out_shape=(jax.ShapeDtypeStruct((rows, columns), B...  2.83 us

profile of v5, /device:TPU:0, one launch (start us, length us, event | category | flops | bytes accessed | tf_op | source)
XLA Modules:
  0.0 37.5 jit_solution(15882036836987746131)
XLA Ops:
  1.3 33.4 %shard_map.147 = (bf16[256,512]{1,0:T(8,128)(2,1)S(1)}, bf16[256,512]{1,0:T(8,128)(2,1)S(1)}, bf16[1024,2048]{1,0:T(8,128)(2,1)S(1)}, f32[4,4,128]{2,1,0:T(4,128)S(1)}) custom-call(bf16[1024,2048]{1,0:T(8,128)(2,1)} %residual.1, f32[1,2048]{1,0:T(1,128)} %bitcast.9, bf16[2048,512]{1,0:T(8,128)(2,1)} %key_weight.1, bf16[2048,512]{1,0:T(8,128)(2,1)} %value_weight.1, ...), custom_call_target="tpu_custom_call" | custom-call | tf_op jit(solution)/shard_map/pallas_call | solution.py:453
  34.7 2.8 %shard_map.148 = (bf16[256,512]{1,0:T(8,128)(2,1)}, bf16[256,512]{1,0:T(8,128)(2,1)}, bf16[1024,2048]{1,0:T(8,128)(2,1)}, f32[4,4]{1,0:T(4,128)}) custom-call(bf16[256,512]{1,0:T(8,128)(2,1)S(1)} %get-tuple-element.8.key_in, bf16[256,512]{1,0:T(8,128)(2,1)S(1)} %get-tuple-element.9.value_in, bf16[1024,2048]{1,0:T(8,128)(2,1)S(1)} %get-tuple-element.10.hidden_in, ...), custom_call_target="tpu_custom_call" | custom-call | tf_op jit(solution)/shard_map/pallas_call | solution.py:524
